TPU v7x, 32 devices: a whole 2x2x4 slice. The times are simulated.
32 devices in a mesh: dp: 8 (over y, x, core), seq: 4 (over z).
Axes of the slice: x: 2, y: 2, z: 4, core: 2. Of those that a mesh axis runs over, the one named last changes fastest.
Arguments:
- tokens: bfloat16 [16384, 768], P(('dp', 'seq')), may hold values from -6 to 6
- w_qkv: bfloat16 [768, 2304], P(('dp', 'seq')), may hold values from -0.21875 to 0.21875
- w_out: bfloat16 [768, 768], P(('dp', 'seq')), may hold values from -1.75 to 1.75
- attn_gain: bfloat16 [768], P(('dp', 'seq')), may hold values from 0.5 to 1.5
- mlp_gain: bfloat16 [768], P(('dp', 'seq')), may hold values from 0.5 to 1.5
- w_in: bfloat16 [768, 2, 1152], P('dp', None, 'seq'), may hold values from -0.21875 to 0.21875
- w_down: bfloat16 [1152, 768], P('seq', 'dp'), may hold values from -0.1875 to 0.1875
- grad_out: bfloat16 [16384, 768], P(('dp', 'seq')), may hold values from -6 to 6
Outputs:
- out_block: bfloat16 [16384, 768], P(('dp', 'seq'))
- grad_tokens: bfloat16 [16384, 768], P(('dp', 'seq'))
- grad_w_qkv: float32 [768, 2304], P(('dp', 'seq'))
- grad_w_out: float32 [768, 768], P(('dp', 'seq'))
- grad_attn_gain: float32 [768], P(('dp', 'seq'))
- grad_mlp_gain: float32 [768], P(('dp', 'seq'))
- grad_w_in: float32 [768, 2, 1152], P('dp', None, 'seq')
- grad_w_down: float32 [1152, 768], P('seq', 'dp')
All inputs are finite; a program needn't handle non-finite values.
Results may differ from a plain program's by a relative error of at most 0.028.
Values may be sent and summed in bfloat16 or wider, within the bound.
A program may use at most 128 MiB of HBM per device.

v0:
```python
import functools
import math

import jax
import jax.numpy as jnp
import numpy as np
from jax import lax
from jax.experimental import pallas as pl
from jax.experimental.pallas import tpu as pltpu
from jax.sharding import PartitionSpec as P

HEADS = 12
HEAD_DIM = 64
NORM_EPS = 1e-05
ROPE_THETA = 160000.0

F32 = jnp.float32
BF = jnp.bfloat16
MESH = pl.DeviceIdType.MESH
NT = (((1,), (1,)), ((), ()))
NN = (((1,), (0,)), ((), ()))
TN = (((0,), (0,)), ((), ()))

WIDTH = 768
PAIRS = HEADS // 2
UNITS = 1152
GROUPS = 8
LINE = 4
BAND = WIDTH // GROUPS
SLIVER = BAND // LINE
SHARE = UNITS // LINE
MAIN = 256
REST = SHARE - MAIN
LINKED = (0, 1, 3, 2)
HALF = WIDTH // 2
CUTS = {640: 256, 512: 256, 896: 384}
LOG2E = math.log2(math.e)
SCALE = HEAD_DIM**-0.5


def dot(a, b, dims):
    return lax.dot_general(a, b, dims, preferred_element_type=F32)


def lanes_of(tile, width=128):
    return pl.ds(pl.multiple_of(tile * width, width), width)


def tiles(start, width):
    return pl.ds(pl.multiple_of(start, width if width < 128 else 128), width)


def lane_iota():
    return lax.broadcasted_iota(jnp.int32, (1, 128), 1)


def swap_halves(u):
    low = lax.rem(lane_iota(), 64) < 32
    return jnp.where(low, pltpu.roll(u, 96, 1), pltpu.roll(u, 32, 1))


def rope(u, cos, sine):
    return u * cos + swap_halves(u) * sine


def rope_back(u, cos, sine):
    return u * cos - swap_halves(u) * sine


def rope_tables(rows):
    position = np.arange(rows, dtype=np.float32)
    half = HEAD_DIM // 2
    freq = (ROPE_THETA ** (-np.arange(half) * 2.0 / HEAD_DIM)).astype(np.float32)
    angle = (position[:, None] * freq[None, :]).astype(np.float64)
    cos, sine = np.cos(angle), np.sin(angle)
    return np.concatenate([cos, cos, -sine, sine], 1).astype(np.float32)


def spread_tables(cos, sine):
    low = lane_iota() < 64

    def chunk(c, _):
        both = cos[c]
        other = pltpu.roll(both, 64, 1)
        cos[c] = jnp.where(low, both, other)
        sine[c] = jnp.where(low, other, both)
        return 0

    lax.fori_loop(0, cos.shape[0], chunk, 0)


def normed(x):
    centred = x - jnp.mean(x, -1, keepdims=True)
    inv = lax.rsqrt(jnp.mean(centred * centred, -1, keepdims=True) + NORM_EPS)
    return centred * inv, inv


def norm_back(dy, gain, hat, inv):
    d = dy * gain
    return inv * (d - jnp.mean(d, -1, keepdims=True) - hat * jnp.mean(d * hat, -1, keepdims=True))


def remote(src, dst, send, recv, device):
    return pltpu.make_async_remote_copy(src, dst, send, recv, device_id=device, device_id_type=MESH)


class Place:
    def __init__(self, nz):
        self.dp, self.z = lax.axis_index("dp"), lax.axis_index("seq")
        self.nz = nz
        upper = self.z // (nz // 2)
        self.moves = lax.rem(self.dp, 2) != upper
        self.stays = lax.rem(self.dp, 2) == upper
        self.shard = jnp.where(self.moves, nz - 1 - self.z, self.z)
        self.opposite = {"dp": self.dp ^ 1, "seq": nz - 1 - self.z}
        self.twin = {"dp": self.dp ^ 1}
        self.beside = {"seq": self.z ^ 1}

    def greet(self, masks):
        bar = pltpu.get_barrier_semaphore()

        def hello(device):
            pl.semaphore_signal(bar, inc=1, device_id=device, device_id_type=MESH)

        for o in range(1, self.nz):
            hello({"seq": lax.rem(self.z + o, self.nz)})
        for m in masks:
            hello({"dp": self.dp ^ m})
        hello(self.opposite)
        pl.semaphore_wait(bar, self.nz + len(masks))


class Gather:
    COPIES = 9

    def __init__(self, src, out, cut, nz, masks, send, recv):
        self.src, self.out, self.cut, self.nz, self.masks = src, out, cut, nz, masks
        self.send, self.recv = send, recv
        self.dp, self.z = lax.axis_index("dp"), lax.axis_index("seq")
        self.started = []
        self.relayed = None

    @staticmethod
    def sems(nz):
        return Gather.COPIES * nz + nz

    def key(self, o, k):
        return o * self.COPIES + k

    def copy(self, src, dst, device, k):
        return remote(src, dst, self.send.at[k], self.recv.at[k], device)

    def begin(self, src, dst, device, k, p=None):
        self.copy(src, dst, device, k).start()
        self.started.append((k, p))

    def arrived(self, ref, k):
        self.copy(ref, ref, {"dp": self.dp ^ self.masks[0]}, k).wait_recv()

    def slot(self, o):
        return self.z ^ LINKED[o]

    def part(self, ref, p):
        if p is None:
            return ref
        width = self.out.shape[-1]
        return ref.at[:, pl.ds(0, self.cut)] if p == 0 else ref.at[:, pl.ds(self.cut, width - self.cut)]

    def along(self, o):
        self.begin(self.src, self.out.at[self.dp, self.z], {"seq": self.z ^ LINKED[o]}, self.COPIES * self.nz + o)

    def relay(self, o):
        ref = self.out.at[self.dp, self.slot(o)]
        self.arrived(ref, self.COPIES * self.nz + o)
        self.relayed = o
        self.begin(ref, ref, {"seq": self.z ^ 1}, self.COPIES * self.nz + 3)

    def forward(self, src, d, s, mask, k, p=None):
        dst = self.out.at[d, s]
        self.begin(self.part(src, p), self.part(dst, p), {"dp": self.dp ^ mask}, k, p)

    def first(self, o):
        my, mx, mc = self.masks
        s = self.slot(o)
        src = self.src
        if o:
            src = self.out.at[self.dp, s]
            if o != self.relayed:
                self.arrived(src, self.COPIES * self.nz + o)
        self.forward(src, self.dp, s, my, self.key(o, 0))
        self.forward(src, self.dp, s, mx, self.key(o, 1))
        self.forward(src, self.dp, s, mc, self.key(o, 2))

    def second(self, o):
        my, mx, mc = self.masks
        s = self.slot(o)
        for m, k, k2, kc, p, m2 in ((my, 0, 3, 4, 0, mx), (mx, 1, 5, 6, 1, my)):
            ref = self.out.at[self.dp ^ m, s]
            self.arrived(ref, self.key(o, k))
            self.forward(ref, self.dp ^ m, s, m2, self.key(o, k2), p)
            self.forward(ref, self.dp ^ m, s, mc, self.key(o, kc))

    def third(self, o):
        my, mx, mc = self.masks
        s = self.slot(o)
        d = self.dp ^ my ^ mx
        for p, k, kc in ((0, 3, 7), (1, 5, 8)):
            ref = self.out.at[d, s]
            self.arrived(self.part(ref, p), self.key(o, k))
            self.forward(ref, d, s, mc, self.key(o, kc), p)

    def finish(self, o):
        my, mx, mc = self.masks
        s = self.slot(o)
        for k, d in ((2, mc), (4, mc ^ my), (6, mc ^ mx)):
            self.arrived(self.out.at[self.dp ^ d, s], self.key(o, k))
        for k, p in ((7, 0), (8, 1)):
            self.arrived(self.part(self.out.at[self.dp ^ mc ^ my ^ mx, s], p), self.key(o, k))

    def done(self):
        for k, p in self.started:
            ref = self.part(self.out.at[self.dp, self.z], p)
            self.copy(ref, ref, {"dp": self.dp ^ self.masks[0]}, k).wait_send()


def pack_group(w, tile, i):
    q, k, v = [w[:, WIDTH * j + HALF * i : WIDTH * j + HALF * i + HALF] for j in range(3)]
    return jnp.concatenate([jnp.concatenate([q, v[:, :256]], 1), jnp.concatenate([k, v[:, 256:], tile], 1)], 0)


def unpack_group(total):
    r = total.shape[0] // 2
    upper, lower = total[:r], total[r:]
    return upper[:, :HALF], lower[:, :HALF], upper[:, HALF:], lower[:, HALF : HALF + 128], lower[:, HALF + 128 :]


def pack_out(w, tile):
    return jnp.concatenate([jnp.concatenate([w[:, :HALF], w[:, HALF:]], 0), jnp.concatenate([tile, jnp.zeros_like(tile)], 0)], 1)


def pack_mlp(gate, up, down):
    parts = (gate, up, down)
    pads = jnp.zeros((gate.shape[0], 128 - 3 * REST), gate.dtype)
    return jnp.concatenate([x[:, :MAIN] for x in parts] + [x[:, MAIN:] for x in parts] + [pads], 1)


def unpack_mlp(total):
    return [
        jnp.concatenate([total[:, MAIN * i : MAIN * i + MAIN], total[:, 3 * MAIN + REST * i : 3 * MAIN + REST * i + REST]], 1)
        for i in range(3)
    ]


def front_kernel(nz, masks, rows, *refs):
    fused = masks is not None
    if fused:
        (tok, gout, w_qkv, w_out, gains, w_in, w_down, cos_in), refs = refs[:8], refs[8:]
    else:
        (tok, gout, g0_all, g1_all, cos_in), refs = refs[:5], refs[5:]
    (mixed, lse, query, gain, tok_own, gout_own, kv, firsts, wqkv), refs = refs[:9], refs[9:]
    if fused:
        (po_all, pm_all), refs = refs[:2], refs[2:]
    (tok_all, kvb, fb, wq, cos, sine, gcol, acc, top, total, tsend, trecv, loc), refs = refs[:13], refs[13:]
    me = Place(nz)
    own = me.shard

    def here(src, dst, k):
        return pltpu.make_async_copy(src, dst, loc.at[k])

    def there(src, dst, device, k):
        return remote(src, dst, tsend.at[k], trecv.at[k], device)

    def rows_to(src, c, device, k, i):
        at = pl.ds(i * (rows // 2), rows // 2)
        src = tok_all.at[c] if src is None else src
        return there(src.at[at], tok_all.at[c, at], device, k + 5 * i)

    @pl.when(me.stays)
    def _():
        here(tok, tok_all.at[own], 0).start()
        here(gout, gout_own, 1).start()

    here(cos_in, cos, 2).start()
    groups, later = [], []
    every, rest = range(nz), (2, 1, 3)
    if fused:
        p0, p1, po, pm, g0_all, g1_all, *sems = refs
        row = lax.broadcasted_iota(jnp.int32, (128, 128), 0)

        def tile_of(i):
            return jnp.where(row == 0, gains[i : i + 1, :], 0.0).T[:SLIVER]

        p0[...] = pack_group(w_qkv[...].astype(F32), tile_of(0), 0).astype(BF)
        g0_all[me.dp, me.z] = p0[...]
    me.greet(masks or (1,))
    if fused:
        shapes = ((p0, g0_all), (p1, g1_all), (po, po_all), (pm, pm_all))
        packs = [
            Gather(src, dst, CUTS[src.shape[-1]], nz, masks, sems[2 * i], sems[2 * i + 1]) for i, (src, dst) in enumerate(shapes)
        ]
        groups, later = packs[:2], packs[2:]
        for o in rest:
            groups[0].along(o)
        groups[0].first(0)

    @pl.when(me.stays)
    def _():
        for i in range(2):
            rows_to(tok, own, me.twin, 1, i).start()
            rows_to(tok, own, me.beside, 2, i).start()

    @pl.when(me.moves)
    def _():
        for i in range(2):
            rows_to(tok, me.z, me.opposite, 0, i).start()

    def swapped(i):
        @pl.when(me.moves)
        def _():
            rows_to(None, own, me.opposite, 0, i).wait_recv()
            rows_to(None, own, me.beside, 2, i).start()
            rows_to(None, own, me.twin, 1, i).start()

    if fused:
        w = w_qkv[...].astype(F32)
        p1[...] = pack_group(w, jnp.zeros((SLIVER, 128), F32), 1).astype(BF)
        g1_all[me.dp, me.z] = p1[...]
        po[...] = pack_out(w_out[...].astype(F32), tile_of(1)).astype(BF)
        w = w_in[...].astype(F32)
        pm[...] = pack_mlp(w[:, :SHARE], w[:, SHARE:], w_down[...].astype(F32).T).astype(BF)
        here(po, po_all.at[me.dp, me.z], 4).start()
        here(pm, pm_all.at[me.dp, me.z], 5).start()
        for o in rest:
            groups[1].along(o)
        groups[1].first(0)
        groups[0].second(0)
        for o in rest:
            groups[0].first(o)
        swapped(0)
        for o in rest:
            groups[0].second(o)
        for o in rest:
            groups[1].first(o)
        for g in later:
            g.along(1)
            g.first(0)

    if not fused:
        swapped(0)
    swapped(1)

    @pl.when(me.stays)
    def _():
        here(tok, tok_all.at[own], 0).wait()

    here(tok_all.at[own], tok_own, 6).start()
    if fused:
        for g in later:
            g.along(2)
        for o in range(nz):
            groups[0].third(o)
        for o in range(nz):
            groups[0].finish(o)

    @pl.when(me.moves)
    def _():
        there(gout, gout_own, me.opposite, 4).start()

    here(cos_in, cos, 2).wait()
    spread_tables(cos, sine)

    def build(i, whole):
        def band_of(g, _):
            slabs = [unpack_group(whole[g, s].astype(F32)) for s in range(LINE)]
            band = pl.ds(pl.multiple_of(g * BAND, BAND), BAND)
            q, k, v0, v1, t = [jnp.concatenate([x[j] for x in slabs], 0) for j in range(5)]
            at = WIDTH * i
            wq[band, at : at + HALF] = k.astype(BF)
            wq[band, at + HALF : at + HALF + 256] = v0.astype(BF)
            wq[band, at + HALF + 256 : at + WIDTH] = v1.astype(BF)
            wq[band, 2 * WIDTH + HALF * i : 2 * WIDTH + HALF * i + HALF] = q.astype(BF)
            if i == 0:
                gcol[band, :] = t
            return 0

        lax.fori_loop(0, GROUPS, band_of, 0)

    def norm_chunk(c):
        def block(i, _):
            at = pl.ds(pl.multiple_of(i * 64, 64), 64)
            hat, _ = normed(tok_all[c, at, :].astype(F32))
            fb[c, at, :] = (hat * gain[0:1, :]).astype(BF)
            return 0

        lax.fori_loop(0, rows // 64, block, 0)
        here(fb.at[c], firsts.at[c], 8 + c).start()

    def queries(i):
        u = dot(fb[own], wq[:, 2 * WIDTH + HALF * i : 2 * WIDTH + HALF * i + HALF], NN)
        for j in range(3):
            tile = rope(u[:, 128 * j : 128 * j + 128], cos[own], sine[own])
            query[:, HALF * i + 128 * j : HALF * i + 128 * j + 128] = (tile * (SCALE * LOG2E)).astype(BF)

    def visits(steps):
        def visit(n, _):
            t, grp = lax.rem(n, nz), n // nz
            stay = jnp.where(t == 1, 1, jnp.where(t == 2, 3, 2))
            move = jnp.where(t == 1, 3, jnp.where(t == 2, 2, 1))
            turn = jnp.where(me.stays, stay, move)
            c = jnp.where(t == 0, own, own ^ turn)
            @pl.when((n > 0) & (n < nz))
            def _():
                for i in range(2):
                    rows_to(None, c, me.twin, jnp.where(turn == 1, 2, jnp.where(turn == 3, 1, 3)), i).wait_recv()

                    @pl.when(turn == 1)
                    def _(i=i):
                        rows_to(None, c, me.twin, 3, i).start()

                norm_chunk(c)

            for j in range(3):
                u = dot(fb[c], wq[:, tiles(WIDTH * grp + 256 * j, 256)], NN)
                for i in range(2):
                    tile = 2 * j + i
                    x = u[:, 128 * i : 128 * i + 128]
                    x = rope(x, cos[c], sine[c]) if tile < 3 else x
                    kvb[grp, c, :, 128 * tile : 128 * tile + 128] = x.astype(BF)
            here(kvb.at[grp, c], kv.at[grp, c], 8 + nz * (1 + grp) + c).start()
            jobs = [(i, h) for i in range(3) for h in range(2)]

            def score(i, h):
                q = query[:, tiles(HALF * grp + 128 * i, 128)]
                mask = (lane_iota() < 64) if h == 0 else (lane_iota() >= 64)
                return dot(kvb[grp, c, :, 128 * i : 128 * i + 128], jnp.where(mask, q, jnp.zeros_like(q)), NT)

            ready = [score(*j) for j in jobs[:2]]
            for m, (i, h) in enumerate(jobs):
                if h == 0:
                    vt = kvb[grp, c, :, HALF + 128 * i : HALF + 128 * i + 128].T
                s = ready[m]
                if m + 2 < len(jobs):
                    ready.append(score(*jobs[m + 2]))
                head = pl.ds(6 * grp + m, 1)
                band = tiles(64 * (6 * grp + m), 64)
                old = top[head, :]
                new = jnp.maximum(old, jnp.max(s, 0, keepdims=True))
                p = jnp.exp2(s - new)
                fade = jnp.exp2(old - new)
                top[head, :] = new
                lhs = jnp.concatenate([vt[h * 64 : h * 64 + 64], jnp.ones((16, rows), BF)], 0)
                oo = dot(lhs, p.astype(BF), NN)
                total[head, :] = total[head, :] * fade + oo[64:65]
                acc[band, :] = acc[band, :] * fade + oo[:64]
            for k, step in steps.items():

                @pl.when(n == k)
                def _(k=k, step=step):
                    for which, name, order in step:
                        for g in which:
                            for o in order:
                                getattr(g, name)(o)
                    if k == nz - 1:
                        build(1, g1_all)
                        here(wq, wqkv, 7).start()
                        queries(1)

            return 0

        lax.fori_loop(0, 2 * nz, visit, 0)

    build(0, g0_all)
    gain[...] = gcol[...].T[:8]
    norm_chunk(own)
    queries(0)
    acc[...] = jnp.zeros_like(acc)
    total[...] = jnp.zeros_like(total)
    top[...] = jnp.full_like(top, -1e30)
    one = groups[1:]
    visits({
        0: [(one, "second", every), (later, "first", (1,))],
        1: [(one, "third", every)],
        2: [(later, "relay", (2,)), (later, "first", (2,))],
        3: [(one, "finish", every), (later, "second", (0, 1))],
        4: [(later, "first", (3,))],
        5: [(later, "second", (2,))],
        6: [(later, "second", (3,))],
        7: [(later, "third", every)],
    })

    for hp in range(PAIRS):
        parts = [
            acc[128 * hp + 64 * h : 128 * hp + 64 * h + 64, :] / total[2 * hp + h : 2 * hp + h + 1, :] for h in range(2)
        ]
        mixed[:, 128 * hp : 128 * hp + 128] = jnp.concatenate(parts, 0).T.astype(BF)
    lse[...] = top[...] + jnp.log(jnp.maximum(total[...], 1e-30)) * LOG2E

    if fused:
        for g in later:
            for o in range(nz):
                g.finish(o)
        for g in packs:
            g.done()
        here(po, po_all.at[me.dp, me.z], 4).wait()
        here(pm, pm_all.at[me.dp, me.z], 5).wait()
    for i in range(2):
        for k in (1, 2, 3):
            rows_to(None, own, me.twin, k, i).wait_send()

    @pl.when(me.moves)
    def _():
        for i in range(2):
            rows_to(None, own, me.opposite, 0, i).wait_send()
        there(gout, gout_own, me.opposite, 4).wait()

    @pl.when(me.stays)
    def _():
        here(gout, gout_own, 1).wait()

    here(tok_all.at[own], tok_own, 6).wait()
    here(wq, wqkv, 7).wait()
    for c in range(nz):
        here(fb.at[c], firsts.at[c], 8 + c).wait()
        for grp in range(2):
            here(kvb.at[grp, c], kv.at[grp, c], 8 + nz * (1 + grp) + c).wait()


def front(tok, gout, weights, tables, nz, masks):
    rows = tok.shape[0]
    vmem, anyspace = pl.BlockSpec(memory_space=pltpu.VMEM), pl.BlockSpec(memory_space=pl.ANY)
    shape, vm = jax.ShapeDtypeStruct, pltpu.VMEM
    outs = [shape((rows, WIDTH), BF), shape((16, rows), F32), shape((rows, WIDTH), BF), shape((8, WIDTH), F32)]
    outs += [shape((rows, WIDTH), BF)] * 2
    outs += [shape((2, nz, rows, WIDTH), BF), shape((nz, rows, WIDTH), BF), shape((WIDTH, 3 * WIDTH), BF)]
    out_specs = [vmem] * 4 + [anyspace, vmem] + [anyspace] * 3
    scratch = [
        vm((nz, rows, WIDTH), BF),
        vm((2, nz, rows, WIDTH), BF),
        vm((nz, rows, WIDTH), BF),
        vm((WIDTH, 3 * WIDTH), BF),
        vm((nz, rows, 128), F32),
        vm((nz, rows, 128), F32),
        vm((WIDTH, 128), F32),
        vm((WIDTH, rows), F32),
        vm((16, rows), F32),
        vm((16, rows), F32),
        pltpu.SemaphoreType.DMA((9,)),
        pltpu.SemaphoreType.DMA((9,)),
        pltpu.SemaphoreType.DMA((8 + 3 * nz,)),
    ]
    if masks:
        grp, out, mlp = (2 * SLIVER, 640), (2 * SLIVER, 512), (BAND, 896)
        outs += [shape((GROUPS, nz) + out, BF), shape((GROUPS, nz) + mlp, BF)]
        out_specs += [anyspace] * 2
        scratch += [vm(x, BF) for x in (grp, grp, out, mlp)] + [vm((GROUPS, nz) + grp, BF)] * 2
        scratch += [pltpu.SemaphoreType.DMA((Gather.sems(nz),)) for _ in range(8)]
    return pl.pallas_call(
        functools.partial(front_kernel, nz, masks, rows),
        out_shape=outs,
        in_specs=[anyspace] * 2 + [vmem] * len(weights) + [anyspace],
        out_specs=out_specs,
        scratch_shapes=scratch,
        compiler_params=pltpu.CompilerParams(collective_id=0, has_side_effects=True, vmem_limit_bytes=60 << 20),
        cost_estimate=pl.CostEstimate(flops=14_000_000_000, bytes_accessed=40_000_000, transcendentals=13_000_000),
        name="front",
    )(tok, gout, *weights, tables)


def middle_kernel(rows, tok, mixed, gout, po_all, pm_all, out, gmid, gmixed, delta, po_g, pm_g,
                  wout, wg, wu, wd, gcol, gain, resid, hat, inv, second, hidden, ggate, gup, gsec, gattn, dwout):
    lane = lane_iota()

    def build(g, _):
        band = pl.ds(pl.multiple_of(g * BAND, BAND), BAND)
        slabs = [po_all[g, s].astype(F32) for s in range(LINE)]
        wout[band, :384] = jnp.concatenate([x[:SLIVER, :384] for x in slabs], 0).astype(BF)
        wout[band, 384:] = jnp.concatenate([x[SLIVER:, :384] for x in slabs], 0).astype(BF)
        gcol[band, :] = jnp.concatenate([x[:SLIVER, 384:] for x in slabs], 0)
        for i, w in enumerate((wg, wu, wd)):
            tail = jnp.zeros((BAND, 128), F32)
            for s in range(LINE):
                w[band, MAIN * s : MAIN * s + MAIN] = pm_all[g, s, :, MAIN * i : MAIN * i + MAIN]
                rest = pm_all[g, s, :, 3 * MAIN :].astype(F32)
                turn = (REST * (s - i)) % 128
                rest = pltpu.roll(rest, turn, 1) if turn else rest
                tail = jnp.where((lane >= REST * s) & (lane < REST * (s + 1)), rest, tail)
            w[band, MAIN * LINE :] = tail.astype(BF)
        return 0

    lax.fori_loop(0, GROUPS, build, 0)
    gain[...] = gcol[...].T[:8]

    for j in range(3):
        at = slice(256 * j, 256 * j + 256)
        resid[:, at] = tok[:, at].astype(F32) + dot(mixed[...], wout[:, at], NN)

    def norm_block(i, _):
        at = pl.ds(pl.multiple_of(i * 64, 64), 64)
        h, r = normed(resid[at, :])
        hat[at, :] = h
        inv[at, :] = jnp.broadcast_to(r, (64, 128))
        second[at, :] = (h * gain[0:1, :]).astype(BF)
        return 0

    lax.fori_loop(0, rows // 64, norm_block, 0)

    def units(start, width):
        at = pl.ds(start, width)
        gate, up, gh = dot(second[...], wg[:, at], NN), dot(second[...], wu[:, at], NN), dot(gout[...], wd[:, at], NN)
        cdf = 0.5 + 0.5 * lax.erf(gate * math.sqrt(0.5))
        pdf = jnp.exp2(gate * gate * (-0.5 * LOG2E)) * (1.0 / math.sqrt(2.0 * math.pi))
        act = gate * cdf
        hidden[:, at] = (act * up).astype(BF)
        gup[:, at] = (gh * act).astype(BF)
        ggate[:, at] = (gh * up * (cdf + gate * pdf)).astype(BF)

    for start in range(0, UNITS, 256):
        units(start, min(256, UNITS - start))

    for j in range(3):
        at = slice(256 * j, 256 * j + 256)
        out[:, at] = (resid[:, at] + dot(hidden[...], wd[at, :], NT)).astype(BF)
        gsec[:, at] = dot(ggate[...], wg[at, :], NT) + dot(gup[...], wu[at, :], NT)

    def back_block(i, dgain):
        at = pl.ds(pl.multiple_of(i * 64, 64), 64)
        dy, h = gsec[at, :], hat[at, :]
        gm = gout[at, :].astype(F32) + norm_back(dy, gain[0:1, :], h, inv[at, 0:1])
        gmid[at, :] = gm
        gattn[at, :] = gm.astype(BF)
        return dgain + jnp.sum(dy * h, 0, keepdims=True)

    dgain = lax.fori_loop(0, rows // 64, back_block, jnp.zeros((1, WIDTH), F32))

    heads = lax.broadcasted_iota(jnp.int32, (16, 256), 0)
    for j in range(3):
        at = slice(256 * j, 256 * j + 256)
        gmx = dot(gattn[...], wout[at, :], NT).astype(BF)
        gmixed[:, at] = gmx
        prod = gmx.astype(F32) * mixed[:, at].astype(F32)
        high = prod.astype(BF)
        low = (prod - high.astype(F32)).astype(BF)
        pick = ((lax.broadcasted_iota(jnp.int32, (16, 256), 1) + 256 * j) // HEAD_DIM == heads).astype(BF)
        part = dot(pick, high, NT) + dot(pick, low, NT)
        delta[...] = part if j == 0 else delta[...] + part

    for j in range(2):
        at = slice(384 * j, 384 * j + 384)
        dwout[at, :] = dot(mixed[:, at], gattn[...], TN)
    row = lax.broadcasted_iota(jnp.int32, (128, WIDTH), 0)
    gcol[...] = jnp.where(row == 0, dgain, 0.0).T

    def pack_out(g, _):
        for s in range(LINE):
            at = pl.ds(pl.multiple_of(g * BAND + s * SLIVER, 8), SLIVER)
            x, c = dwout[at, :], gcol[at, :]
            po_g[g, s, :, :384] = jnp.concatenate([x[:, :384], x[:, 384:]], 0).astype(BF)
            po_g[g, s, :, 384:] = jnp.concatenate([c, jnp.zeros_like(c)], 0).astype(BF)
        return 0

    lax.fori_loop(0, GROUPS, pack_out, 0)

    for j in range(2):
        at = slice(384 * j, 384 * j + 384)
        tails = []
        for i, (a, b) in enumerate(((second, ggate), (second, gup), (gout, hidden))):
            for s in range(LINE):
                x = dot(a[:, at], b[:, MAIN * s : MAIN * s + MAIN], TN).astype(BF)
                for g in range(4):
                    pm_g[4 * j + g, s, :, MAIN * i : MAIN * i + MAIN] = x[BAND * g : BAND * g + BAND]
            tails.append(dot(a[:, at], b[:, MAIN * LINE :], TN))
        for s in range(LINE):
            y = jnp.zeros((384, 128), F32)
            for i, tail in enumerate(tails):
                turn = (REST * (i - s)) % 128
                tail = pltpu.roll(tail, turn, 1) if turn else tail
                y = jnp.where((lane >= REST * i) & (lane < REST * (i + 1)), tail, y)
            y = y.astype(BF)
            for g in range(4):
                pm_g[4 * j + g, s, :, 3 * MAIN :] = y[BAND * g : BAND * g + BAND]


def middle(tok, mixed, gout, po_all, pm_all):
    rows = tok.shape[0]
    shape, vm = jax.ShapeDtypeStruct, pltpu.VMEM
    vmem = pl.BlockSpec(memory_space=pltpu.VMEM)
    return pl.pallas_call(
        functools.partial(middle_kernel, rows),
        out_shape=[
            shape((rows, WIDTH), BF),
            shape((rows, WIDTH), F32),
            shape((rows, WIDTH), BF),
            shape((16, rows), F32),
            shape(po_all.shape, BF),
            shape(pm_all.shape, BF),
        ],
        in_specs=[vmem] * 5,
        out_specs=[vmem] * 6,
        scratch_shapes=[
            vm((WIDTH, WIDTH), BF),
            vm((WIDTH, UNITS), BF),
            vm((WIDTH, UNITS), BF),
            vm((WIDTH, UNITS), BF),
            vm((WIDTH, 128), F32),
            vm((8, WIDTH), F32),
            vm((rows, WIDTH), F32),
            vm((rows, WIDTH), F32),
            vm((rows, 128), F32),
            vm((rows, WIDTH), BF),
            vm((rows, UNITS), BF),
            vm((rows, UNITS), BF),
            vm((rows, UNITS), BF),
            vm((rows, WIDTH), F32),
            vm((rows, WIDTH), BF),
            vm((WIDTH, WIDTH), F32),
        ],
        compiler_params=pltpu.CompilerParams(vmem_limit_bytes=58 << 20),
        cost_estimate=pl.CostEstimate(flops=11_000_000_000, bytes_accessed=25_000_000, transcendentals=1_200_000),
        name="middle",
    )(tok, mixed, gout, po_all, pm_all)


class Reduce:
    COPIES = 10

    def __init__(self, src, total, cut, nz, masks, bufs, send, recv, loc=None):
        self.src, self.total, self.cut, self.nz, self.masks = src, total, cut, nz, masks
        self.near, self.side0, self.side1, self.far, *mine = bufs
        self.mine = mine[0] if mine else None
        self.send, self.recv, self.loc = send, recv, loc
        self.dp, self.z = lax.axis_index("dp"), lax.axis_index("seq")
        my, mx, mc = masks
        self.turns = (0, my, mx, my ^ mx)
        self.started = []

    @staticmethod
    def scratch(shape, nz, held):
        r, c = shape
        cut = CUTS[c]
        bufs = [
            pltpu.VMEM((4, nz, r, c), BF),
            pltpu.VMEM((3, nz, r, cut), BF),
            pltpu.VMEM((3, nz, r, c - cut), BF),
            pltpu.VMEM((nz - 1, r, c), BF),
        ]
        sems = [pltpu.SemaphoreType.DMA((Reduce.COPIES * nz + nz,))] * 2
        if not held:
            bufs += [pltpu.VMEM((4, nz, r, c), BF)]
            sems += [pltpu.SemaphoreType.DMA((4 * nz,))]
        return bufs, sems

    def begin(self, src, dst, device, k):
        remote(src, dst, self.send.at[k], self.recv.at[k], device).start()
        self.started.append((k, src.shape[-1]))

    def arrived(self, ref, k):
        remote(ref, ref, self.send.at[k], self.recv.at[k], {"dp": self.dp ^ self.masks[2]}).wait_recv()

    def seat(self, o):
        return self.z ^ LINKED[o]

    def held(self, i, s):
        return self.mine.at[i, s] if self.mine is not None else self.src.at[self.dp ^ self.turns[i], s]

    def local(self, i, o):
        s = self.seat(o)
        return pltpu.make_async_copy(self.src.at[self.dp ^ self.turns[i], s], self.mine.at[i, s], self.loc.at[4 * o + i])

    def zero(self, o):
        s, mc = self.seat(o), self.masks[2]
        for i in (3, 1, 2, 0):
            if self.mine is not None:
                self.local(i, o).start()
            self.begin(self.src.at[self.dp ^ mc ^ self.turns[i], s], self.near.at[i, s], {"dp": self.dp ^ mc}, self.COPIES * o + i)

    def add(self, ref, other):
        ref[...] = (ref[...].astype(F32) + other[...].astype(F32)).astype(BF)

    def p0(self, i, s):
        return self.held(i, s).at[:, pl.ds(0, self.cut)]

    def p1(self, i, s):
        return self.held(i, s).at[:, pl.ds(self.cut, self.src.shape[-1] - self.cut)]

    def one(self, o):
        my, mx, _ = self.masks
        s, k = self.seat(o), self.COPIES * o
        for i in (3, 1, 2, 0):
            if self.mine is not None:
                self.local(i, o).wait()
            self.arrived(self.near.at[i, s], k + i)
            self.add(self.held(i, s), self.near.at[i, s])
            if i == 3:
                self.begin(self.p0(3, s), self.side0.at[1, s], {"dp": self.dp ^ my}, k + 4)
                self.begin(self.p1(3, s), self.side1.at[1, s], {"dp": self.dp ^ mx}, k + 5)
            if i == 1:
                self.begin(self.p0(1, s), self.side0.at[0, s], {"dp": self.dp ^ my}, k + 6)
            if i == 2:
                self.begin(self.p1(2, s), self.side1.at[0, s], {"dp": self.dp ^ mx}, k + 7)

    def two(self, o):
        my, mx, _ = self.masks
        s, k = self.seat(o), self.COPIES * o
        self.arrived(self.side0.at[1, s], k + 4)
        self.add(self.p0(2, s), self.side0.at[1, s])
        self.begin(self.p0(2, s), self.side0.at[2, s], {"dp": self.dp ^ mx}, k + 8)
        self.arrived(self.side1.at[1, s], k + 5)
        self.add(self.p1(1, s), self.side1.at[1, s])
        self.begin(self.p1(1, s), self.side1.at[2, s], {"dp": self.dp ^ my}, k + 9)

    def three(self, o):
        s, k = self.seat(o), self.COPIES * o
        for ref, side, k1, k2 in ((self.p0(0, s), self.side0, k + 6, k + 8), (self.p1(0, s), self.side1, k + 7, k + 9)):
            self.arrived(side.at[0, s], k1)
            self.arrived(side.at[2, s], k2)
            ref[...] = (ref[...].astype(F32) + side[0, s].astype(F32) + side[2, s].astype(F32)).astype(BF)
        if o:
            self.begin(self.held(0, s), self.far.at[o - 1], {"seq": s}, self.COPIES * self.nz + o)

    def four(self):
        out = self.held(0, self.z)[...].astype(F32)
        for o in range(1, self.nz):
            self.arrived(self.far.at[o - 1], self.COPIES * self.nz + o)
            out = out + self.far[o - 1].astype(F32)
        self.total[...] = out

    def done(self):
        for k, width in self.started:
            whole = width == self.src.shape[-1]
            ref = self.near.at[0, 0] if whole else (self.side0 if k % self.COPIES in (4, 6, 8) else self.side1).at[0, 0]
            remote(ref, ref, self.send.at[k], self.recv.at[k], {"dp": self.dp ^ self.masks[2]}).wait_send()


def back_kernel(nz, masks, rows, *refs):
    fused = masks is not None
    (tok, gmid, out_own, query, kv, firsts, wqkv, gain, gmixed, lse, delta, cos_in), refs = refs[:12], refs[12:]
    if fused:
        (po_g, pm_g, gtok, out, s0, s1, so, sm), refs = refs[:8], refs[8:]
    else:
        (gtok, out, p0_g, p1_g), refs = refs[:4], refs[4:]
    (kvb, fb, ft, wq, cos, sine, dq, dqb, dkv, dx, dw, sent, landed, gown, gcol, send, recv, loc), refs = refs[:18], refs[18:]
    me = Place(nz)
    own = me.shard

    def here(src, dst, k):
        return pltpu.make_async_copy(src, dst, loc.at[k])

    def there(src, dst, device, k):
        return remote(src, dst, send.at[k], recv.at[k], device)

    def chunk(t):
        return jnp.where(t == 0, own ^ 2, jnp.where(t == 1, own ^ 1, jnp.where(t == 2, own ^ 3, own)))

    def fetch(n):
        return here(kv.at[n // nz, chunk(lax.rem(n, nz))], kvb.at[lax.rem(n, 2)], lax.rem(n, 2))

    def fetch_first(t):
        return here(firsts.at[chunk(t)], fb.at[lax.rem(t, 2)], 2 + lax.rem(t, 2))

    fetch(0).start()
    fetch_first(0).start()
    whole = [here(wqkv, wq, 4), here(cos_in, cos, 5)]
    for c in whole:
        c.start()
    me.greet(masks or (1,))
    jobs, sums = [], []
    if fused:
        (p0_g, p1_g), refs = refs[:2], refs[2:]
        for src, total in ((p0_g, s0), (p1_g, s1)):
            sums.append(Reduce(src, total, CUTS[src.shape[-1]], nz, masks, refs[:4], *refs[4:6]))
            refs = refs[6:]
        for src, total in ((po_g, so), (pm_g, sm)):
            jobs.append(Reduce(src, total, CUTS[src.shape[-1]], nz, masks, refs[:5], *refs[5:8]))
            refs = refs[8:]
    order = (3, 2, 1, 0)

    def advance(which, step):
        for j in which:
            for o in order:
                getattr(j, step)(o)

    def wave(which):
        for i in range(nz + 2):
            for k, step in enumerate(("one", "two", "three")):
                if 0 <= i - k < nz:
                    for j in which:
                        getattr(j, step)(order[i - k])

    advance(jobs, "zero")

    @pl.when(me.moves)
    def _():
        there(out_own, out, me.opposite, 3).start()

    @pl.when(me.stays)
    def _():
        here(out_own, out, 7).start()

    dq[...] = jnp.zeros_like(dq)
    for c in whole:
        c.wait()
    spread_tables(cos, sine)

    def visits(steps):
        def visit(n, _):
            t, grp = lax.rem(n, nz), n // nz
            c, slot = chunk(t), lax.rem(t, 2)
            fetch(n).wait()

            @pl.when(n < nz)
            def _():
                fetch_first(t).wait()

            @pl.when(n + 1 < 2 * nz)
            def _():
                fetch(n + 1).start()

            @pl.when(n + 1 < nz)
            def _():
                fetch_first(n + 1).start()

            band = pl.ds(pl.multiple_of(t * rows, rows), rows)
            todo = [(i, h) for i in range(3) for h in range(2)]

            def pick(ref, i, h):
                x = ref[:, tiles(HALF * grp + 128 * i, 128)]
                mask = (lane_iota() < 64) if h == 0 else (lane_iota() >= 64)
                return jnp.where(mask, x, jnp.zeros_like(x))

            def score(i, h):
                qh, gh = pick(query, i, h), pick(gmixed, i, h)
                k, v = kvb[slot, :, 128 * i : 128 * i + 128], kvb[slot, :, HALF + 128 * i : HALF + 128 * i + 128]
                return dot(k, qh, NT), dot(v, gh, NT), qh, gh

            ready = [score(*todo[0])]
            dk = dv = None
            for m, (i, h) in enumerate(todo):
                s, dp, qh, gh = ready[m]
                if m + 1 < len(todo):
                    ready.append(score(*todo[m + 1]))
                if h == 0:
                    kt = kvb[slot, :, 128 * i : 128 * i + 128].T
                head = pl.ds(6 * grp + m, 1)
                rows_of = tiles(64 * (6 * grp + m), 64)
                p = jnp.exp2(s - lse[head, :])
                ds = (p * (dp - delta[head, :])).astype(BF)
                a = dot(p.astype(BF), gh, NN)
                dv = a if h == 0 else dv + a
                a = dot(ds, qh, NN)
                dk = a if h == 0 else dk + a
                dq[rows_of, :] += dot(kt[h * 64 : h * 64 + 64], ds, NN)
                if h == 1:
                    at = WIDTH * grp + 128 * i
                    dkv[band, tiles(at, 128)] = rope_back(dk * (1.0 / LOG2E), cos[c], sine[c]).astype(BF)
                    dkv[band, tiles(at + HALF, 128)] = dv.astype(BF)

            @pl.when(n < nz)
            def _():
                for j in range(6):
                    ft[128 * j : 128 * j + 128, band] = fb[slot, :, 128 * j : 128 * j + 128].T
            @pl.when(n >= nz)
            def _():
                for j in range(3):
                    at = slice(256 * j, 256 * j + 256)
                    dx[:, at] = dot(dkv[band, :], wq[at, : 2 * WIDTH], NT)

                @pl.when(lax.rem(t, 2) == 0)
                def _():
                    sent[t] = dx[...].astype(BF)
                    there(sent.at[t], landed.at[t], me.twin, t).start()

                @pl.when(t == 1)
                def _():
                    there(sent.at[0], landed.at[0], me.twin, 0).wait_recv()
                    sent[1] = (dx[...] + landed[0].astype(F32)).astype(BF)
                    there(sent.at[1], landed.at[1], me.beside, 1).start()

            for k, step in steps.items():

                @pl.when(n == k)
                def _(k=k, step=step):
                    if k == nz - 1:
                        close(0)
                        weigh(0)
                        pack(0, p0_g)
                    for which, name in step:
                        advance(which, name)

            return 0

        lax.fori_loop(0, 2 * nz, visit, 0)

    def close(grp):
        for i in range(3 * grp, 3 * grp + 3):
            at = slice(128 * i, 128 * i + 128)
            dqb[:, at] = rope_back(dq[at, :].T * SCALE, cos[own], sine[own]).astype(BF)

    def weigh(grp):
        for r in (slice(0, HALF), slice(HALF, WIDTH)):
            for j in range(3):
                at = WIDTH * grp + 256 * j
                dw[r, HALF + 256 * j : HALF + 256 * j + 256] = dot(ft[r, :], dkv[:, at : at + 256], NN)
            dw[r, :HALF] = dot(ft[r, (nz - 1) * rows :], dqb[:, HALF * grp : HALF * grp + HALF], NN)

    def pack(grp, dst):
        def band_of(g, _):
            for s in range(LINE):
                at = pl.ds(pl.multiple_of(g * BAND + s * SLIVER, 8), SLIVER)
                q, k, v0, v1 = dw[at, :HALF], dw[at, HALF:WIDTH], dw[at, WIDTH : WIDTH + 256], dw[at, WIDTH + 256 :]
                tile = gcol[at, :] if grp else jnp.zeros((SLIVER, 128), F32)
                dst[g, s] = jnp.concatenate(
                    [jnp.concatenate([q, v0], 1), jnp.concatenate([k, v1, tile], 1)], 0
                ).astype(BF)
            return 0

        lax.fori_loop(0, GROUPS, band_of, 0)

    early = sums[:1]
    visits({
        0: [(jobs, "one")],
        3: [(early, "zero")],
        4: [(jobs, "two"), (early, "one")],
        6: [(jobs, "three")],
        7: [(early, "two"), (early, "three")],
    })
    close(1)
    for j in range(3):
        at = slice(256 * j, 256 * j + 256)
        dx[:, at] += dot(dqb[...], wq[at, 2 * WIDTH :], NT)
    there(sent.at[1], landed.at[1], me.beside, 1).wait_recv()
    there(sent.at[2], landed.at[2], me.twin, 2).wait_recv()

    def norm_block(i, dgain):
        at = pl.ds(pl.multiple_of(i * 64, 64), 64)
        dy = dx[at, :] + landed[1, at, :].astype(F32) + landed[2, at, :].astype(F32)
        h, r = normed(tok[at, :].astype(F32))
        gown[at, :] = (gmid[at, :] + norm_back(dy, gain[0:1, :], h, r)).astype(BF)
        return dgain + jnp.sum(dy * h, 0, keepdims=True)

    dgain = lax.fori_loop(0, rows // 64, norm_block, jnp.zeros((1, WIDTH), F32))

    @pl.when(me.moves)
    def _():
        there(gown, gtok, me.opposite, 4).start()

    @pl.when(me.stays)
    def _():
        here(gown, gtok, 8).start()

    row = lax.broadcasted_iota(jnp.int32, (128, WIDTH), 0)
    gcol[...] = jnp.where(row == 0, dgain, 0.0).T
    weigh(1)
    pack(1, p1_g)
    if fused:
        advance(sums[1:], "zero")
        wave(sums[1:])
        for j in jobs + sums:
            j.four()
        for j in jobs + sums:
            j.done()
    for k, device in ((0, me.twin), (1, me.beside), (2, me.twin)):
        there(sent.at[k], landed.at[k], device, k).wait_send()

    @pl.when(me.moves)
    def _():
        there(out_own, out, me.opposite, 3).wait()
        there(gown, gtok, me.opposite, 4).wait()

    @pl.when(me.stays)
    def _():
        here(out_own, out, 7).wait()
        here(gown, gtok, 8).wait()


def back(tok, gmid, out_own, query, kv, firsts, wqkv, gain, gmixed, lse, delta, tables, packs, nz, masks):
    rows = tok.shape[0]
    shape, vm = jax.ShapeDtypeStruct, pltpu.VMEM
    vmem, anyspace = pl.BlockSpec(memory_space=pltpu.VMEM), pl.BlockSpec(memory_space=pl.ANY)
    in_specs = [vmem] * 4 + [anyspace] * 3 + [vmem] * 4 + [anyspace]
    slab = (2 * SLIVER, 640)
    outs, out_specs = [shape((rows, WIDTH), BF)] * 2, [vmem] * 2
    scratch = [
        vm((2, rows, WIDTH), BF),
        vm((2, rows, WIDTH), BF),
        vm((WIDTH, nz * rows), BF),
        vm((WIDTH, 3 * WIDTH), BF),
        vm((nz, rows, 128), F32),
        vm((nz, rows, 128), F32),
        vm((WIDTH, rows), F32),
        vm((rows, WIDTH), BF),
        vm((nz * rows, 2 * WIDTH), BF),
        vm((rows, WIDTH), F32),
        vm((WIDTH, 3 * HALF), F32),
        vm((3, rows, WIDTH), BF),
        vm((3, rows, WIDTH), BF),
        vm((rows, WIDTH), BF),
        vm((WIDTH, 128), F32),
        pltpu.SemaphoreType.DMA((5,)),
        pltpu.SemaphoreType.DMA((5,)),
        pltpu.SemaphoreType.DMA((9,)),
    ]
    if masks:
        in_specs += [anyspace] * 2
        outs += [shape(s, F32) for s in (slab, slab, packs[0].shape[-2:], packs[1].shape[-2:])]
        out_specs += [vmem] * 4
        scratch += [vm((GROUPS, LINE) + slab, BF)] * 2
        for s, held in ((slab, True), (slab, True), (packs[0].shape[-2:], False), (packs[1].shape[-2:], False)):
            bufs, sems = Reduce.scratch(s, nz, held)
            scratch += bufs + sems
    else:
        outs += [shape((GROUPS, LINE) + slab, BF)] * 2
        out_specs += [vmem] * 2
        packs = []
    return pl.pallas_call(
        functools.partial(back_kernel, nz, masks, rows),
        out_shape=outs,
        in_specs=in_specs,
        out_specs=out_specs,
        scratch_shapes=scratch,
        compiler_params=pltpu.CompilerParams(collective_id=1, has_side_effects=True, vmem_limit_bytes=62 << 20),
        cost_estimate=pl.CostEstimate(flops=24_000_000_000, bytes_accessed=40_000_000, transcendentals=13_000_000),
        name="back",
    )(tok, gmid, out_own, query, kv, firsts, wqkv, gain, gmixed, lse, delta, tables, *packs)


def finish_kernel(out, gtok, s0, s1, so, sm, out_o, gtok_o, qkv_o, w_out_o, gains_o, gate_o, down_o):
    out_o[...] = out[...]
    gtok_o[...] = gtok[...]
    for i, total in enumerate((s0, s1)):
        q, k, v0, v1, tile = unpack_group(total[...])
        for j, x in enumerate((q, k)):
            qkv_o[:, WIDTH * j + HALF * i : WIDTH * j + HALF * i + HALF] = x
        at = 2 * WIDTH + HALF * i
        qkv_o[:, at : at + 256] = v0
        qkv_o[:, at + 256 : at + HALF] = v1
    w_out_o[:, :HALF] = so[:SLIVER, :HALF]
    w_out_o[:, HALF:] = so[SLIVER:, :HALF]
    zeros = jnp.zeros((128 - SLIVER, 128), F32)
    for i, col in enumerate((tile, so[:SLIVER, HALF:])):
        gains_o[i : i + 1, :] = jnp.concatenate([col, zeros], 0).T[:1]
    gate, up, down = unpack_mlp(sm[...])
    gate_o[:, :SHARE] = gate
    gate_o[:, SHARE:] = up
    down_o[...] = down.T


def finish(out, gtok, s0, s1, so, sm):
    shape = jax.ShapeDtypeStruct
    vmem = pl.BlockSpec(memory_space=pltpu.VMEM)
    return pl.pallas_call(
        finish_kernel,
        out_shape=[
            shape(out.shape, BF),
            shape(gtok.shape, BF),
            shape((SLIVER, 3 * WIDTH), F32),
            shape((SLIVER, WIDTH), F32),
            shape((8, 128), F32),
            shape((BAND, 2 * SHARE), F32),
            shape((SHARE, BAND), F32),
        ],
        in_specs=[vmem] * 6,
        out_specs=[vmem] * 7,
        compiler_params=pltpu.CompilerParams(vmem_limit_bytes=40 << 20),
        name="finish",
    )(out, gtok, s0, s1, so, sm)


def whole_packs(w_qkv, w_out, attn_gain, mlp_gain, w_in, w_down):
    both = ("dp", "seq")

    def shards_of(w):
        w = lax.all_gather(w, both, axis=0, tiled=True)
        return w.reshape(GROUPS * LINE, SLIVER, -1)

    def slabs(pack, w, gain):
        found = jax.vmap(pack)(w, jnp.pad(gain, ((0, 0), (0, 0), (0, 127))))
        return found.reshape((GROUPS, LINE) + found.shape[1:])

    qkv, gain_a, gain_m = shards_of(w_qkv), shards_of(attn_gain), shards_of(mlp_gain)
    groups = [slabs(lambda w, t, i=i: pack_group(w, t, i), qkv, gain_a) for i in range(2)]
    w_in, w_down = lax.all_gather(w_in, "dp", axis=0, tiled=True), lax.all_gather(w_down, "dp", axis=1, tiled=True)
    mlp = lax.all_gather(pack_mlp(w_in[:, 0], w_in[:, 1], w_down.T), "seq", axis=0, tiled=False)
    mlp = mlp.reshape(LINE, GROUPS, BAND, -1).transpose(1, 0, 2, 3)
    return groups, slabs(pack_out, shards_of(w_out), gain_m), mlp


def whole_sums(p0_g, p1_g, po_g, pm_g):
    both = ("dp", "seq")

    def scattered(x):
        return lax.psum_scatter(x.reshape(WIDTH, -1), both, scatter_dimension=0, tiled=True)

    parts = [jax.vmap(unpack_group)(p.reshape((GROUPS * LINE,) + p.shape[2:]).astype(F32)) for p in (p0_g, p1_g)]
    columns = [parts[0][0], parts[1][0], parts[0][1], parts[1][1], parts[0][2], parts[0][3], parts[1][2], parts[1][3]]
    g_qkv, gain_a = scattered(jnp.concatenate(columns, -1)), scattered(parts[1][4][..., :1])[:, 0]
    po = po_g.reshape(GROUPS * LINE, 2 * SLIVER, -1).astype(F32)
    g_out = scattered(jnp.concatenate([po[:, :SLIVER, :HALF], po[:, SLIVER:, :HALF]], -1))
    gain_m = scattered(po[:, :SLIVER, HALF : HALF + 1])[:, 0]
    mlp = pm_g.astype(F32).transpose(1, 0, 2, 3).reshape(LINE, WIDTH, -1)
    mlp = lax.psum_scatter(mlp, "seq", scatter_dimension=0, tiled=False)
    gate, up, down = unpack_mlp(lax.psum_scatter(mlp, "dp", scatter_dimension=0, tiled=True))
    return g_qkv, g_out, gain_a, gain_m, jnp.stack([gate, up], 1), down.T


def on_device(tokens, w_qkv, w_out, attn_gain, mlp_gain, w_in, w_down, grad_out, *, dp, nz):
    rows = tokens.shape[0]
    masks = (dp // 2, dp // 4, 1) if dp == GROUPS else None
    tables = jnp.asarray(rope_tables(nz * rows)).reshape(nz, rows, 128)
    if masks:
        gains = jnp.pad(jnp.stack([attn_gain, mlp_gain]).astype(F32), ((0, 6), (0, 128 - SLIVER)))
        weights = [w_qkv, w_out, gains, w_in.reshape(w_in.shape[0], -1), w_down]
        got = front(tokens, grad_out, weights, tables, nz, masks)
        po_all, pm_all = got[-2:]
    else:
        groups, po_all, pm_all = whole_packs(w_qkv, w_out, attn_gain, mlp_gain, w_in, w_down)
        got = front(tokens, grad_out, groups, tables, nz, None)
    mixed, lse, query, gain, tok_own, gout_own, kv, firsts, wqkv = got[:9]
    out_own, gmid, gmixed, delta, po_g, pm_g = middle(tok_own, mixed, gout_own, po_all, pm_all)
    found = back(tok_own, gmid, out_own, query, kv, firsts, wqkv, gain, gmixed, lse, delta, tables, [po_g, pm_g], nz, masks)
    gtok, out, *sums = found
    if not masks:
        return (out, gtok, *whole_sums(*sums, po_g, pm_g))
    out, gtok, g_qkv, g_out, gains, g_in, g_down = finish(out, gtok, *sums)
    g_in = g_in.reshape(g_in.shape[0], 2, SHARE)
    return out, gtok, g_qkv, g_out, gains[0, :SLIVER], gains[1, :SLIVER], g_in, g_down


def solution(mesh):
    both = P(("dp", "seq"), None)
    vector = P(("dp", "seq"))
    w_in, w_down = P("dp", None, "seq"), P("seq", "dp")
    step = functools.partial(on_device, dp=mesh.shape["dp"], nz=mesh.shape["seq"])
    return jax.shard_map(
        step,
        mesh=mesh,
        in_specs=(both, both, both, vector, vector, w_in, w_down, both),
        out_specs=(both, both, both, both, vector, vector, w_in, w_down),
        check_vma=False,
    )
```

profile of v0, /device:TPU:0, one launch (start us, length us, event | category | flops | bytes accessed | tf_op | source)
XLA Modules:
  0.0 221.9 jit_solution(1071344199452144270)
XLA Ops:
  0.6 1.3 fusion.6.refs_4_
  1.9 1.7 reshape.25.refs_5_
  3.6 81.7 %front.1 = (bf16[512,768]{1,0:T(8,128)(2,1)}, f32[16,512]{1,0:T(8,128)}, bf16[512,768]{1,0:T(8,128)(2,1)}, f32[8,768]{1,0:T(8,128)}, bf16[512,768]{1,0:T(8,128)(...) custom-call(bf16[512,768]{1,0:T(8,128)(2,1)} %refs_0_.1, ...), custom_call_target="tpu_custom_call" | custom-call | flops 14000000000 | bytes 40000000 | tf_op jit(solution)/shard_map/front/pallas_call | solution.py:557
  85.3 24.6 %middle.1 = (bf16[512,768]{1,0:T(8,128)(2,1)}, f32[512,768]{1,0:T(8,128)}, bf16[512,768]{1,0:T(8,128)(2,1)}, f32[16,512]{1,0:T(8,128)}, bf16[8,4,48,512]{3,2,1,0...) custom-call(bf16[512,768]{1,0:T(8,128)(2,1)} %get-tuple-element.38.tok.refs_0_, bf16[512,768]{1,0:T(8,128)(2,1)} %get-tuple-element.39.mixed, ...), custom_call_target="tpu_custom_call" | custom-call | flops 11000000512 | bytes 25000000 | tf_op jit(solution)/shard_map/middle/pallas_call | solution.py:687
  110.0 103.1 %back.1 = (bf16[512,768]{1,0:T(8,128)(2,1)}, bf16[512,768]{1,0:T(8,128)(2,1)}, f32[48,640]{1,0:T(8,128)}, f32[48,640]{1,0:T(8,128)}, f32[48,512]{1,0:T(8,128)}, /*index=5*/f32[96,896]{1,0:T(8,128)}) custom-call(bf16[512,768]{1,0:T(8,128)(2,1)} %get-tuple-element.38.tok.refs_0_, f32[512,768]{1,0:T(8,128)} %get-tuple-element.43.refs_1_, ...), custom_call_target="tpu_custom_call" | custom-call | flops 24000000000 | bytes 40000000 | tf_op jit(solution)/shard_map/back/pallas_call | solution.py:1114
  213.0 0.0 copy-start
  213.0 1.1 copy-done
  214.1 0.0 copy-start.1
  214.2 1.1 copy-done.1
  215.3 0.0 copy-start.2
  215.3 1.0 copy-done.2
  216.3 0.0 copy-start.3
  216.3 0.9 copy-done.3
  217.2 0.0 copy-start.4
  217.2 0.9 copy-done.4
  218.1 0.0 copy-start.5
  218.1 0.9 copy-done.5
  219.0 1.5 finish.1
  220.4 0.5 slice_bitcast_fusion
  220.9 0.9 reshape.27
Async XLA Ops:
  213.0 1.1 copy-start
  214.1 1.1 copy-start.1
  215.3 1.0 copy-start.2
  216.3 0.9 copy-start.3
  217.2 0.9 copy-start.4
  218.1 0.9 copy-start.5
where the time goes:
time: 222 us
  Pallas kernels  211 us (95%)
  local copies, waits for them, and re-layouts  9.11 us (4%)
    pallas_call x1, Pallas kernels, back(): pl.pallas_call(functools.partial(back_kernel, nz, masks, rows), out_shape...  103 us
    pallas_call x1, Pallas kernels, front(): pl.pallas_call(functools.partial(front_kernel, nz, masks, rows), out_shap...  81.7 us
    pallas_call x1, Pallas kernels, middle(): pl.pallas_call(functools.partial(middle_kernel, rows), out_shape=[shape((...  24.6 us
    unnamed x12, local copies, waits for them, and re-layouts  5.93 us

commit v1 on v0

--- a/solution.py
+++ b/solution.py
@@ -254,7 +254,7 @@
 def front_kernel(nz, masks, rows, *refs):
     fused = masks is not None
     if fused:
-        (tok, gout, w_qkv, w_out, gains, w_in, w_down, cos_in), refs = refs[:8], refs[8:]
+        (tok, gout, w_qkv, w_out, gain_a, gain_m, w_in, w_down, cos_in), refs = refs[:9], refs[9:]
     else:
         (tok, gout, g0_all, g1_all, cos_in), refs = refs[:5], refs[5:]
     (mixed, lse, query, gain, tok_own, gout_own, kv, firsts, wqkv), refs = refs[:9], refs[9:]
@@ -287,10 +287,11 @@
         p0, p1, po, pm, g0_all, g1_all, *sems = refs
         row = lax.broadcasted_iota(jnp.int32, (128, 128), 0)
 
-        def tile_of(i):
-            return jnp.where(row == 0, gains[i : i + 1, :], 0.0).T[:SLIVER]
-
-        p0[...] = pack_group(w_qkv[...].astype(F32), tile_of(0), 0).astype(BF)
+        def tile_of(part):
+            line = jnp.concatenate([part[...].astype(F32), jnp.zeros((1, 128 - SLIVER), F32)], 1)
+            return jnp.where(row == 0, line, 0.0).T[:SLIVER]
+
+        p0[...] = pack_group(w_qkv[...].astype(F32), tile_of(gain_a), 0).astype(BF)
         g0_all[me.dp, me.z] = p0[...]
     me.greet(masks or (1,))
     if fused:
@@ -325,9 +326,8 @@
         w = w_qkv[...].astype(F32)
         p1[...] = pack_group(w, jnp.zeros((SLIVER, 128), F32), 1).astype(BF)
         g1_all[me.dp, me.z] = p1[...]
-        po[...] = pack_out(w_out[...].astype(F32), tile_of(1)).astype(BF)
-        w = w_in[...].astype(F32)
-        pm[...] = pack_mlp(w[:, :SHARE], w[:, SHARE:], w_down[...].astype(F32).T).astype(BF)
+        po[...] = pack_out(w_out[...].astype(F32), tile_of(gain_m)).astype(BF)
+        pm[...] = pack_mlp(w_in[:, 0, :].astype(F32), w_in[:, 1, :].astype(F32), w_down[...].astype(F32).T).astype(BF)
         here(po, po_all.at[me.dp, me.z], 4).start()
         here(pm, pm_all.at[me.dp, me.z], 5).start()
         for o in rest:
@@ -1123,7 +1123,7 @@
     )(tok, gmid, out_own, query, kv, firsts, wqkv, gain, gmixed, lse, delta, tables, *packs)
 
 
-def finish_kernel(out, gtok, s0, s1, so, sm, out_o, gtok_o, qkv_o, w_out_o, gains_o, gate_o, down_o):
+def finish_kernel(out, gtok, s0, s1, so, sm, out_o, gtok_o, qkv_o, w_out_o, gain_a_o, gain_m_o, w_in_o, down_o):
     out_o[...] = out[...]
     gtok_o[...] = gtok[...]
     for i, total in enumerate((s0, s1)):
@@ -1136,11 +1136,11 @@
     w_out_o[:, :HALF] = so[:SLIVER, :HALF]
     w_out_o[:, HALF:] = so[SLIVER:, :HALF]
     zeros = jnp.zeros((128 - SLIVER, 128), F32)
-    for i, col in enumerate((tile, so[:SLIVER, HALF:])):
-        gains_o[i : i + 1, :] = jnp.concatenate([col, zeros], 0).T[:1]
+    for dst, col in ((gain_a_o, tile), (gain_m_o, so[:SLIVER, HALF:])):
+        dst[...] = jnp.concatenate([col, zeros], 0).T[:1, :SLIVER]
     gate, up, down = unpack_mlp(sm[...])
-    gate_o[:, :SHARE] = gate
-    gate_o[:, SHARE:] = up
+    w_in_o[:, 0, :] = gate
+    w_in_o[:, 1, :] = up
     down_o[...] = down.T
 
 
@@ -1154,13 +1154,14 @@
             shape(gtok.shape, BF),
             shape((SLIVER, 3 * WIDTH), F32),
             shape((SLIVER, WIDTH), F32),
-            shape((8, 128), F32),
-            shape((BAND, 2 * SHARE), F32),
+            shape((1, SLIVER), F32),
+            shape((1, SLIVER), F32),
+            shape((BAND, 2, SHARE), F32),
             shape((SHARE, BAND), F32),
         ],
         in_specs=[vmem] * 6,
-        out_specs=[vmem] * 7,
-        compiler_params=pltpu.CompilerParams(vmem_limit_bytes=40 << 20),
+        out_specs=[vmem] * 8,
+        compiler_params=pltpu.CompilerParams(vmem_limit_bytes=60 << 20),
         name="finish",
     )(out, gtok, s0, s1, so, sm)
 
@@ -1207,8 +1208,7 @@
     masks = (dp // 2, dp // 4, 1) if dp == GROUPS else None
     tables = jnp.asarray(rope_tables(nz * rows)).reshape(nz, rows, 128)
     if masks:
-        gains = jnp.pad(jnp.stack([attn_gain, mlp_gain]).astype(F32), ((0, 6), (0, 128 - SLIVER)))
-        weights = [w_qkv, w_out, gains, w_in.reshape(w_in.shape[0], -1), w_down]
+        weights = [w_qkv, w_out, attn_gain[None], mlp_gain[None], w_in, w_down]
         got = front(tokens, grad_out, weights, tables, nz, masks)
         po_all, pm_all = got[-2:]
     else:
@@ -1220,9 +1220,8 @@
     gtok, out, *sums = found
     if not masks:
         return (out, gtok, *whole_sums(*sums, po_g, pm_g))
-    out, gtok, g_qkv, g_out, gains, g_in, g_down = finish(out, gtok, *sums)
-    g_in = g_in.reshape(g_in.shape[0], 2, SHARE)
-    return out, gtok, g_qkv, g_out, gains[0, :SLIVER], gains[1, :SLIVER], g_in, g_down
+    out, gtok, g_qkv, g_out, gain_a, gain_m, g_in, g_down = finish(out, gtok, *sums)
+    return out, gtok, g_qkv, g_out, gain_a[0], gain_m[0], g_in, g_down
 
 
 def solution(mesh):

time: 222 us -> 214 us (0.964)
  local copies, waits for them, and re-layouts: 9.11 us -> 0 us
    unnamed x12 -> x0, local copies, waits for them, and re-layouts: 5.93 us -> none
    reshape x2 -> x0, local copies, waits for them, and re-layouts: 2.66 us -> none  [the longest x1 1.71 us: on_device(): weights = [w_qkv, w_out, gains, w_in.reshape(w_in.shape[0], -1), w_down]]
where the time goes in v1:
time: 214 us; the launch traced here: 213 us
  Pallas kernels  213 us (100%)
    pallas_call x1, Pallas kernels, back(): pl.pallas_call(functools.partial(back_kernel, nz, masks, rows), out_shape...  103 us
    pallas_call x1, Pallas kernels, front(): pl.pallas_call(functools.partial(front_kernel, nz, masks, rows), out_shap...  81.8 us
    pallas_call x1, Pallas kernels, middle(): pl.pallas_call(functools.partial(middle_kernel, rows), out_shape=[shape((...  24.6 us

profile of v1, /device:TPU:0, one launch (start us, length us, event | category | flops | bytes accessed | tf_op | source)
XLA Modules:
  0.0 213.4 jit_solution(164707590922065963)
XLA Ops:
  0.6 81.8 %front.1 = (bf16[512,768]{1,0:T(8,128)(2,1)}, f32[16,512]{1,0:T(8,128)}, bf16[512,768]{1,0:T(8,128)(2,1)}, f32[8,768]{1,0:T(8,128)}, bf16[512,768]{1,0:T(8,128)(...) custom-call(bf16[512,768]{1,0:T(8,128)(2,1)} %refs_0_.1, ...), custom_call_target="tpu_custom_call" | custom-call | flops 14000000000 | bytes 40000000 | tf_op jit(solution)/shard_map/front/pallas_call | solution.py:557
  82.4 24.6 %middle.1 = (bf16[512,768]{1,0:T(8,128)(2,1)}, f32[512,768]{1,0:T(8,128)}, bf16[512,768]{1,0:T(8,128)(2,1)}, f32[16,512]{1,0:T(8,128)}, bf16[8,4,48,512]{3,2,1,0...) custom-call(bf16[512,768]{1,0:T(8,128)(2,1)} %get-tuple-element.39.tok.refs_0_, bf16[512,768]{1,0:T(8,128)(2,1)} %get-tuple-element.40.mixed, ...), custom_call_target="tpu_custom_call" | custom-call | flops 11000000512 | bytes 25000000 | tf_op jit(solution)/shard_map/middle/pallas_call | solution.py:687
  107.1 103.1 %back.1 = (bf16[512,768]{1,0:T(8,128)(2,1)}, bf16[512,768]{1,0:T(8,128)(2,1)}, f32[48,640]{1,0:T(8,128)}, f32[48,640]{1,0:T(8,128)}, f32[48,512]{1,0:T(8,128)}, /*index=5*/f32[96,896]{1,0:T(8,128)}) custom-call(bf16[512,768]{1,0:T(8,128)(2,1)} %get-tuple-element.39.tok.refs_0_, f32[512,768]{1,0:T(8,128)} %get-tuple-element.44.refs_1_, ...), custom_call_target="tpu_custom_call" | custom-call | flops 24000000000 | bytes 40000000 | tf_op jit(solution)/shard_map/back/pallas_call | solution.py:1114
  210.1 3.1 %finish.1 = (bf16[512,768]{1,0:T(8,128)(2,1)}, bf16[512,768]{1,0:T(8,128)(2,1)}, f32[24,2304]{1,0:T(8,128)}, f32[24,768]{1,0:T(8,128)}, f32[1,24]{1,0:T(1,128)},...) custom-call(bf16[512,768]{1,0:T(8,128)(2,1)} %get-tuple-element.56.out, ...), custom_call_target="tpu_custom_call" | custom-call | tf_op jit(solution)/shard_map/finish/pallas_call | solution.py:1150

commit v2 on v1

--- a/solution.py
+++ b/solution.py
@@ -566,9 +566,14 @@
     )(tok, gout, *weights, tables)
 
 
-def middle_kernel(rows, tok, mixed, gout, po_all, pm_all, out, gmid, gmixed, delta, po_g, pm_g,
-                  wout, wg, wu, wd, gcol, gain, resid, hat, inv, second, hidden, ggate, gup, gsec, gattn, dwout):
+def middle_kernel(rows, tok, mixed, gout, po_all, pm_in, out_own, gmid_own, gmixed, delta, po_g, pm_sums,
+                  pm_all, pm_g, out, gmid, loc, wout, wg, wu, wd, gcol, gain, resid, hat, inv, second, hidden, ggate, gup, gsec, gattn, dwout):
     lane = lane_iota()
+
+    def here(src, dst, k):
+        return pltpu.make_async_copy(src, dst, loc.at[k])
+
+    here(pm_in, pm_all, 0).start()
 
     def build(g, _):
         band = pl.ds(pl.multiple_of(g * BAND, BAND), BAND)
@@ -576,6 +581,10 @@
         wout[band, :384] = jnp.concatenate([x[:SLIVER, :384] for x in slabs], 0).astype(BF)
         wout[band, 384:] = jnp.concatenate([x[SLIVER:, :384] for x in slabs], 0).astype(BF)
         gcol[band, :] = jnp.concatenate([x[:SLIVER, 384:] for x in slabs], 0)
+        return 0
+
+    def build_units(g, _):
+        band = pl.ds(pl.multiple_of(g * BAND, BAND), BAND)
         for i, w in enumerate((wg, wu, wd)):
             tail = jnp.zeros((BAND, 128), F32)
             for s in range(LINE):
@@ -603,6 +612,8 @@
         return 0
 
     lax.fori_loop(0, rows // 64, norm_block, 0)
+    here(pm_in, pm_all, 0).wait()
+    lax.fori_loop(0, GROUPS, build_units, 0)
 
     def units(start, width):
         at = pl.ds(start, width)
@@ -622,43 +633,7 @@
         out[:, at] = (resid[:, at] + dot(hidden[...], wd[at, :], NT)).astype(BF)
         gsec[:, at] = dot(ggate[...], wg[at, :], NT) + dot(gup[...], wu[at, :], NT)
 
-    def back_block(i, dgain):
-        at = pl.ds(pl.multiple_of(i * 64, 64), 64)
-        dy, h = gsec[at, :], hat[at, :]
-        gm = gout[at, :].astype(F32) + norm_back(dy, gain[0:1, :], h, inv[at, 0:1])
-        gmid[at, :] = gm
-        gattn[at, :] = gm.astype(BF)
-        return dgain + jnp.sum(dy * h, 0, keepdims=True)
-
-    dgain = lax.fori_loop(0, rows // 64, back_block, jnp.zeros((1, WIDTH), F32))
-
-    heads = lax.broadcasted_iota(jnp.int32, (16, 256), 0)
-    for j in range(3):
-        at = slice(256 * j, 256 * j + 256)
-        gmx = dot(gattn[...], wout[at, :], NT).astype(BF)
-        gmixed[:, at] = gmx
-        prod = gmx.astype(F32) * mixed[:, at].astype(F32)
-        high = prod.astype(BF)
-        low = (prod - high.astype(F32)).astype(BF)
-        pick = ((lax.broadcasted_iota(jnp.int32, (16, 256), 1) + 256 * j) // HEAD_DIM == heads).astype(BF)
-        part = dot(pick, high, NT) + dot(pick, low, NT)
-        delta[...] = part if j == 0 else delta[...] + part
-
-    for j in range(2):
-        at = slice(384 * j, 384 * j + 384)
-        dwout[at, :] = dot(mixed[:, at], gattn[...], TN)
-    row = lax.broadcasted_iota(jnp.int32, (128, WIDTH), 0)
-    gcol[...] = jnp.where(row == 0, dgain, 0.0).T
-
-    def pack_out(g, _):
-        for s in range(LINE):
-            at = pl.ds(pl.multiple_of(g * BAND + s * SLIVER, 8), SLIVER)
-            x, c = dwout[at, :], gcol[at, :]
-            po_g[g, s, :, :384] = jnp.concatenate([x[:, :384], x[:, 384:]], 0).astype(BF)
-            po_g[g, s, :, 384:] = jnp.concatenate([c, jnp.zeros_like(c)], 0).astype(BF)
-        return 0
-
-    lax.fori_loop(0, GROUPS, pack_out, 0)
+    here(out, out_own, 1).start()
 
     for j in range(2):
         at = slice(384 * j, 384 * j + 384)
@@ -678,12 +653,57 @@
             y = y.astype(BF)
             for g in range(4):
                 pm_g[4 * j + g, s, :, 3 * MAIN :] = y[BAND * g : BAND * g + BAND]
+        here(pm_g.at[pl.ds(4 * j, 4)], pm_sums.at[pl.ds(4 * j, 4)], 3 + j).start()
+
+    def back_block(i, dgain):
+        at = pl.ds(pl.multiple_of(i * 64, 64), 64)
+        dy, h = gsec[at, :], hat[at, :]
+        gm = gout[at, :].astype(F32) + norm_back(dy, gain[0:1, :], h, inv[at, 0:1])
+        gmid[at, :] = gm
+        gattn[at, :] = gm.astype(BF)
+        return dgain + jnp.sum(dy * h, 0, keepdims=True)
+
+    dgain = lax.fori_loop(0, rows // 64, back_block, jnp.zeros((1, WIDTH), F32))
+
+    here(gmid, gmid_own, 2).start()
+    heads = lax.broadcasted_iota(jnp.int32, (16, 256), 0)
+    for j in range(3):
+        at = slice(256 * j, 256 * j + 256)
+        gmx = dot(gattn[...], wout[at, :], NT).astype(BF)
+        gmixed[:, at] = gmx
+        prod = gmx.astype(F32) * mixed[:, at].astype(F32)
+        high = prod.astype(BF)
+        low = (prod - high.astype(F32)).astype(BF)
+        pick = ((lax.broadcasted_iota(jnp.int32, (16, 256), 1) + 256 * j) // HEAD_DIM == heads).astype(BF)
+        part = dot(pick, high, NT) + dot(pick, low, NT)
+        delta[...] = part if j == 0 else delta[...] + part
+
+    for j in range(2):
+        at = slice(384 * j, 384 * j + 384)
+        dwout[at, :] = dot(mixed[:, at], gattn[...], TN)
+    row = lax.broadcasted_iota(jnp.int32, (128, WIDTH), 0)
+    gcol[...] = jnp.where(row == 0, dgain, 0.0).T
+
+    def pack_out(g, _):
+        for s in range(LINE):
+            at = pl.ds(pl.multiple_of(g * BAND + s * SLIVER, 8), SLIVER)
+            x, c = dwout[at, :], gcol[at, :]
+            po_g[g, s, :, :384] = jnp.concatenate([x[:, :384], x[:, 384:]], 0).astype(BF)
+            po_g[g, s, :, 384:] = jnp.concatenate([c, jnp.zeros_like(c)], 0).astype(BF)
+        return 0
+
+    lax.fori_loop(0, GROUPS, pack_out, 0)
+
+    here(out, out_own, 1).wait()
+    here(gmid, gmid_own, 2).wait()
+    for j in range(2):
+        here(pm_g.at[pl.ds(4 * j, 4)], pm_sums.at[pl.ds(4 * j, 4)], 3 + j).wait()
 
 
 def middle(tok, mixed, gout, po_all, pm_all):
     rows = tok.shape[0]
     shape, vm = jax.ShapeDtypeStruct, pltpu.VMEM
-    vmem = pl.BlockSpec(memory_space=pltpu.VMEM)
+    vmem, anyspace = pl.BlockSpec(memory_space=pltpu.VMEM), pl.BlockSpec(memory_space=pl.ANY)
     return pl.pallas_call(
         functools.partial(middle_kernel, rows),
         out_shape=[
@@ -694,9 +714,14 @@
             shape(po_all.shape, BF),
             shape(pm_all.shape, BF),
         ],
-        in_specs=[vmem] * 5,
-        out_specs=[vmem] * 6,
+        in_specs=[vmem] * 4 + [anyspace],
+        out_specs=[anyspace, anyspace, vmem, vmem, vmem, anyspace],
         scratch_shapes=[
+            vm(pm_all.shape, BF),
+            vm(pm_all.shape, BF),
+            vm((rows, WIDTH), BF),
+            vm((rows, WIDTH), F32),
+            pltpu.SemaphoreType.DMA((5,)),
             vm((WIDTH, WIDTH), BF),
             vm((WIDTH, UNITS), BF),
             vm((WIDTH, UNITS), BF),

time: 214 us -> 210 us (0.981)
  Pallas kernels: 213 us -> 209 us
    pallas_call x1, Pallas kernels: 24.6 us -> 20.9 us  [middle(): pl.pallas_call(functools.partial(middle_kernel, rows), out_shape=[shape((...]
where the time goes in v2:
time: 210 us
  Pallas kernels  209 us (100%)
    pallas_call x1, Pallas kernels, back(): pl.pallas_call(functools.partial(back_kernel, nz, masks, rows), out_shape...  103 us
    pallas_call x1, Pallas kernels, front(): pl.pallas_call(functools.partial(front_kernel, nz, masks, rows), out_shap...  81.8 us
    pallas_call x1, Pallas kernels, middle(): pl.pallas_call(functools.partial(middle_kernel, rows), out_shape=[shape((...  20.9 us

profile of v2, /device:TPU:0, one launch (start us, length us, event | category | flops | bytes accessed | tf_op | source)
XLA Modules:
  0.0 209.7 jit_solution(17704077504548768168)
XLA Ops:
  0.6 81.8 %front.1 = (bf16[512,768]{1,0:T(8,128)(2,1)}, f32[16,512]{1,0:T(8,128)}, bf16[512,768]{1,0:T(8,128)(2,1)}, f32[8,768]{1,0:T(8,128)}, bf16[512,768]{1,0:T(8,128)(...) custom-call(bf16[512,768]{1,0:T(8,128)(2,1)} %refs_0_.1, ...), custom_call_target="tpu_custom_call" | custom-call | flops 14000000000 | bytes 40000000 | tf_op jit(solution)/shard_map/front/pallas_call | solution.py:557
  82.4 20.9 %middle.1 = (bf16[512,768]{1,0:T(8,128)(2,1)}, f32[512,768]{1,0:T(8,128)}, bf16[512,768]{1,0:T(8,128)(2,1)}, f32[16,512]{1,0:T(8,128)}, bf16[8,4,48,512]{3,2,1,0...) custom-call(bf16[512,768]{1,0:T(8,128)(2,1)} %get-tuple-element.39.tok.refs_0_, bf16[512,768]{1,0:T(8,128)(2,1)} %get-tuple-element.40.mixed, ...), custom_call_target="tpu_custom_call" | custom-call | flops 11000000512 | bytes 25000000 | tf_op jit(solution)/shard_map/middle/pallas_call | solution.py:707
  103.4 103.1 %back.1 = (bf16[512,768]{1,0:T(8,128)(2,1)}, bf16[512,768]{1,0:T(8,128)(2,1)}, f32[48,640]{1,0:T(8,128)}, f32[48,640]{1,0:T(8,128)}, f32[48,512]{1,0:T(8,128)}, /*index=5*/f32[96,896]{1,0:T(8,128)}) custom-call(bf16[512,768]{1,0:T(8,128)(2,1)} %get-tuple-element.39.tok.refs_0_, f32[512,768]{1,0:T(8,128)} %get-tuple-element.44.refs_1_, ...), custom_call_target="tpu_custom_call" | custom-call | flops 24000000000 | bytes 40000000 | tf_op jit(solution)/shard_map/back/pallas_call | solution.py:1139
  206.5 3.1 %finish.1 = (bf16[512,768]{1,0:T(8,128)(2,1)}, bf16[512,768]{1,0:T(8,128)(2,1)}, f32[24,2304]{1,0:T(8,128)}, f32[24,768]{1,0:T(8,128)}, f32[1,24]{1,0:T(1,128)},...) custom-call(bf16[512,768]{1,0:T(8,128)(2,1)} %get-tuple-element.56.out, ...), custom_call_target="tpu_custom_call" | custom-call | tf_op jit(solution)/shard_map/finish/pallas_call | solution.py:1175

commit v3 on v2

--- a/solution.py
+++ b/solution.py
@@ -1101,7 +1101,7 @@
     rows = tok.shape[0]
     shape, vm = jax.ShapeDtypeStruct, pltpu.VMEM
     vmem, anyspace = pl.BlockSpec(memory_space=pltpu.VMEM), pl.BlockSpec(memory_space=pl.ANY)
-    in_specs = [vmem] * 4 + [anyspace] * 3 + [vmem] * 4 + [anyspace]
+    in_specs = [vmem, vmem, anyspace, vmem] + [anyspace] * 3 + [vmem] * 4 + [anyspace]
     slab = (2 * SLIVER, 640)
     outs, out_specs = [shape((rows, WIDTH), BF)] * 2, [vmem] * 2
     scratch = [

time: 210 us -> 210 us (level)
  no operation moved by 1% of the time
where the time goes in v3:
time: 210 us
  Pallas kernels  209 us (100%)
    pallas_call x1, Pallas kernels, back(): pl.pallas_call(functools.partial(back_kernel, nz, masks, rows), out_shape...  103 us
    pallas_call x1, Pallas kernels, front(): pl.pallas_call(functools.partial(front_kernel, nz, masks, rows), out_shap...  81.8 us
    pallas_call x1, Pallas kernels, middle(): pl.pallas_call(functools.partial(middle_kernel, rows), out_shape=[shape((...  20.9 us

profile of v3, /device:TPU:0, one launch (start us, length us, event | category | flops | bytes accessed | tf_op | source)
XLA Modules:
  0.0 209.8 jit_solution(13775918156357949118)
XLA Ops:
  0.6 81.8 %front.1 = (bf16[512,768]{1,0:T(8,128)(2,1)}, f32[16,512]{1,0:T(8,128)}, bf16[512,768]{1,0:T(8,128)(2,1)}, f32[8,768]{1,0:T(8,128)}, bf16[512,768]{1,0:T(8,128)(...) custom-call(bf16[512,768]{1,0:T(8,128)(2,1)} %refs_0_.1, ...), custom_call_target="tpu_custom_call" | custom-call | flops 14000000000 | bytes 40000000 | tf_op jit(solution)/shard_map/front/pallas_call | solution.py:557
  82.4 20.9 %middle.1 = (bf16[512,768]{1,0:T(8,128)(2,1)}, f32[512,768]{1,0:T(8,128)}, bf16[512,768]{1,0:T(8,128)(2,1)}, f32[16,512]{1,0:T(8,128)}, bf16[8,4,48,512]{3,2,1,0...) custom-call(bf16[512,768]{1,0:T(8,128)(2,1)} %get-tuple-element.39.tok.refs_0_, bf16[512,768]{1,0:T(8,128)(2,1)} %get-tuple-element.40.mixed, ...), custom_call_target="tpu_custom_call" | custom-call | flops 11000000512 | bytes 25000000 | tf_op jit(solution)/shard_map/middle/pallas_call | solution.py:707
  103.4 103.1 %back.1 = (bf16[512,768]{1,0:T(8,128)(2,1)}, bf16[512,768]{1,0:T(8,128)(2,1)}, f32[48,640]{1,0:T(8,128)}, f32[48,640]{1,0:T(8,128)}, f32[48,512]{1,0:T(8,128)}, /*index=5*/f32[96,896]{1,0:T(8,128)}) custom-call(bf16[512,768]{1,0:T(8,128)(2,1)} %get-tuple-element.39.tok.refs_0_, f32[512,768]{1,0:T(8,128)} %get-tuple-element.44.refs_1_, ...), custom_call_target="tpu_custom_call" | custom-call | flops 24000000000 | bytes 40000000 | tf_op jit(solution)/shard_map/back/pallas_call | solution.py:1139
  206.5 3.1 %finish.1 = (bf16[512,768]{1,0:T(8,128)(2,1)}, bf16[512,768]{1,0:T(8,128)(2,1)}, f32[24,2304]{1,0:T(8,128)}, f32[24,768]{1,0:T(8,128)}, f32[1,24]{1,0:T(1,128)},...) custom-call(bf16[512,768]{1,0:T(8,128)(2,1)} %get-tuple-element.56.out, ...), custom_call_target="tpu_custom_call" | custom-call | tf_op jit(solution)/shard_map/finish/pallas_call | solution.py:1175
